TPU v7x, 32 devices: a whole 2x2x4 slice. The times are simulated.
32 devices in a mesh: row: 4 (over x, core), col: 8 (over z, y).
Axes of the slice: x: 2, y: 2, z: 4, core: 2. Of those that a mesh axis runs over, the one named last changes fastest.
Arguments:
- vectors: float32 [1792, 128], P('row'), may hold values from -6 to 6
- tiles: float32 [4, 8, 10, 56, 56], P('row', 'col'), may hold values from -0.1875 to 0.1875
- tile_pos: int32 [4, 8, 2, 10], P('row', 'col'), may hold values from 0 to 7
- diag_blocks: float32 [32, 56, 56], P(('row', 'col')), as said below
Outputs:
- filtered: float32 [1792, 128], P('row')
Inputs may be any that keep to these rules, and one draw needn't show every extreme that they name: Where 10 + 1 <= 8, the stored blocks of the device at (r, c) lie in 10 different local block rows, none of them among c * 1 to c + 1 - 1. `diag_blocks`: every diagonal block is symmetric.
All inputs are finite; a program needn't handle non-finite values.
Results may differ from a plain program's by a relative error of at most 0.00011.
Values sent between devices are 32-bit elements; how exact they have to be, the bound alone decides.
A program may use at most 64 MiB of HBM per device.

v0:
```python
import jax
import jax.numpy as jnp
from jax import lax
from jax.sharding import PartitionSpec as P

ORB = 56
DEGREE = 3


filter_low = 0.0
filter_high = 8.0


def body(vectors, tiles, tile_pos, diag_blocks):
    tile_data = tiles[0, 0]
    block_rows = tile_pos[0, 0, 0]
    block_cols = tile_pos[0, 0, 1]
    total_rows, width = vectors.shape
    group_blocks = total_rows // ORB
    slice_blocks = diag_blocks.shape[0]
    slice_rows = slice_blocks * ORB
    column_blocks_n = slice_blocks * lax.axis_size("row")
    start_row = lax.axis_index("col") * slice_rows

    def apply_operator(field):
        own_rows = lax.dynamic_slice_in_dim(field, start_row, slice_rows, 0)
        column_field = lax.all_gather(own_rows, "row", axis=0, tiled=True)
        field_blocks = field.reshape(group_blocks, ORB, width)
        column_blocks = column_field.reshape(column_blocks_n, ORB, width)
        direct = jnp.einsum(
            "tab,tbk->tak", tile_data, column_blocks[block_cols], precision=lax.Precision.HIGHEST
        )
        mirror = jnp.einsum(
            "tba,tbk->tak", tile_data, field_blocks[block_rows], precision=lax.Precision.HIGHEST
        )
        mirror_sum = jax.ops.segment_sum(mirror, block_cols, num_segments=column_blocks_n).reshape(
            column_blocks_n * ORB, width
        )
        own_diag = jnp.einsum(
            "sab,sbk->sak",
            diag_blocks,
            own_rows.reshape(-1, ORB, width),
            precision=lax.Precision.HIGHEST,
        ).reshape(slice_rows, width)
        mirror_own = lax.psum_scatter(mirror_sum, "row", scatter_dimension=0, tiled=True)
        direct_sum = jax.ops.segment_sum(direct, block_rows, num_segments=group_blocks).reshape(
            total_rows, width
        )
        present = lax.dynamic_slice_in_dim(direct_sum, start_row, slice_rows, 0)
        partial_sum = lax.dynamic_update_slice_in_dim(direct_sum, present + own_diag, start_row, 0)
        summed = lax.psum(partial_sum, "col")
        return summed + lax.all_gather(mirror_own, "col", axis=0, tiled=True)

    centre = 0.5 * (filter_high + filter_low)
    half_width = 0.5 * (filter_high - filter_low)
    previous = vectors
    current = (apply_operator(vectors) - centre * vectors) / half_width
    for step in range(DEGREE - 1):
        image = apply_operator(current)
        following = 2.0 * (image - centre * current) / half_width - previous
        previous, current = (current, following)
    return current


def solution(mesh):
    return jax.shard_map(
        body,
        mesh=mesh,
        in_specs=(
            P("row", None),
            P("row", "col", None, None, None),
            P("row", "col", None, None),
            P(("row", "col"), None, None),
        ),
        out_specs=P("row", None),
        check_vma=False,
    )
```

profile of v0, /device:TPU:0, one launch (start us, length us, event | category | flops | bytes accessed | tf_op | source)
XLA Modules:
  0.0 269.6 jit_solution(5590225497959995962)
XLA Ops:
  7.4 0.8 fusion.16
  8.2 1.5 gather_fusion.1
  9.7 0.7 convolution_bitcast_fusion.4
  10.4 1.1 scatter_fusion.1
  11.6 0.6 copy-done.2
  12.2 0.0 all-reduce.7.cloned.1.call-start
  12.3 6.4 %all_gather.18 = f32[224,128]{1,0:T(8,128)S(1)} all-gather(f32[56,128]{1,0:T(8,128)S(1)} %constant_dynamic-slice_fusion.2), channel_id=1, replica_groups=mesh['row'=4,'col'=8] {'row'}, dimensions={0}, use_global_device_ids=true | all-gather | bytes 143360 | tf_op jit(solution)/shard_map/all_gather | solution.py:27
  18.7 0.6 gather_fusion
  19.3 0.6 convolution_bitcast_fusion.5
  19.9 1.1 scatter_fusion
  21.0 0.2 fusion.5
  21.3 0.7 copy-done.5
  22.0 0.0 reduce-scatter.12.cloned.1.call-start
  22.0 12.7 %reduce-scatter.10.cloned.1.call-done = f32[56,128]{1,0:T(8,128)} async-done(((f32[224,128]{1,0:T(8,128)}), f32[56,128]{1,0:T(8,128)}) %reduce-scatter.10.cloned.1.call-update) | async-done | bytes 28688
  34.7 31.0 %all_gather.19 = f32[448,128]{1,0:T(8,128)S(1)} all-gather(f32[56,128]{1,0:T(8,128)} %reduce-scatter.10.cloned.1.call-done), channel_id=1, replica_groups=mesh['row'=4,'col'=8] {'col'}, dimensions={0}, use_global_device_ids=true | all-gather | bytes 258048 | tf_op jit(solution)/shard_map/all_gather | solution.py:52
  65.7 28.2 %all-reduce.7.cloned.1.call-done = f32[448,128]{1,0:T(8,128)} async-done(((f32[448,128]{1,0:T(8,128)}), f32[448,128]{1,0:T(8,128)}) %all-reduce.7.cloned.1.call-update) | async-done | bytes 229392 | tf_op jit(solution)/shard_map/psum | solution.py:51
  94.0 1.0 broadcast_multiply_fusion
  95.0 5.4 %all_gather.20 = f32[224,128]{1,0:T(8,128)S(1)} all-gather(f32[56,128]{1,0:T(8,128)S(1)} %constant_dynamic-slice_fusion), channel_id=1, replica_groups=mesh['row'=4,'col'=8] {'row'}, dimensions={0}, use_global_device_ids=true | all-gather | bytes 143360 | tf_op jit(solution)/shard_map/all_gather | solution.py:27
  100.4 0.6 gather_fusion.2
  101.0 0.6 gather_fusion.3
  101.5 0.7 convolution_bitcast_fusion.2
  102.2 1.1 scatter_fusion.3
  103.4 0.6 copy-done.3
  104.0 0.0 all-reduce.9.cloned.1.call-start
  104.1 0.6 convolution_bitcast_fusion.3
  104.7 1.1 scatter_fusion.2
  105.8 0.2 fusion.3
  106.1 0.7 copy-done.6
  106.8 0.0 reduce-scatter.14.cloned.1.call-start
  106.8 16.1 %reduce-scatter.12.cloned.1.call-done = f32[56,128]{1,0:T(8,128)} async-done(((f32[224,128]{1,0:T(8,128)}), f32[56,128]{1,0:T(8,128)}) %reduce-scatter.12.cloned.1.call-update) | async-done | bytes 28688
  122.9 31.0 %all_gather.21 = f32[448,128]{1,0:T(8,128)S(1)} all-gather(f32[56,128]{1,0:T(8,128)} %reduce-scatter.12.cloned.1.call-done), channel_id=1, replica_groups=mesh['row'=4,'col'=8] {'col'}, dimensions={0}, use_global_device_ids=true | all-gather | bytes 258048 | tf_op jit(solution)/shard_map/all_gather | solution.py:52
  154.0 23.3 %all-reduce.9.cloned.1.call-done = f32[448,128]{1,0:T(8,128)} async-done(((f32[448,128]{1,0:T(8,128)}), f32[448,128]{1,0:T(8,128)}) %all-reduce.9.cloned.1.call-update) | async-done | bytes 229392 | tf_op jit(solution)/shard_map/psum | solution.py:51
  177.3 1.0 multiply_subtract_fusion.1
  178.4 5.4 %all_gather.22 = f32[224,128]{1,0:T(8,128)S(1)} all-gather(f32[56,128]{1,0:T(8,128)S(1)} %constant_dynamic-slice_fusion.1), channel_id=1, replica_groups=mesh['row'=4,'col'=8] {'row'}, dimensions={0}, use_global_device_ids=true | all-gather | bytes 143360 | tf_op jit(solution)/shard_map/all_gather | solution.py:27
  183.7 0.6 gather_fusion.4
  184.3 0.6 gather_fusion.5
  184.9 0.7 convolution_bitcast_fusion
  185.6 1.1 scatter_fusion.5
  186.7 0.6 copy-done.1
  187.4 0.0 all-reduce.11.cloned.1.call-start
  187.4 0.6 convolution_bitcast_fusion.1
  188.1 1.1 scatter_fusion.4
  189.2 0.2 fusion.1
  189.4 0.7 copy-done.4
  190.1 16.2 %reduce-scatter.14.cloned.1.call-done = f32[56,128]{1,0:T(8,128)} async-done(((f32[224,128]{1,0:T(8,128)}), f32[56,128]{1,0:T(8,128)}) %reduce-scatter.14.cloned.1.call-update) | async-done | bytes 28688
  206.3 31.1 %all_gather.23 = f32[448,128]{1,0:T(8,128)S(1)} all-gather(f32[56,128]{1,0:T(8,128)} %reduce-scatter.14.cloned.1.call-done), channel_id=1, replica_groups=mesh['row'=4,'col'=8] {'col'}, dimensions={0}, use_global_device_ids=true | all-gather | bytes 258048 | tf_op jit(solution)/shard_map/all_gather | solution.py:52
  237.4 23.2 %all-reduce.11.cloned.1.call-done = f32[448,128]{1,0:T(8,128)} async-done(((f32[448,128]{1,0:T(8,128)}), f32[448,128]{1,0:T(8,128)}) %all-reduce.11.cloned.1.call-update) | async-done | bytes 229392 | tf_op jit(solution)/shard_map/psum | solution.py:51
  260.6 1.7 multiply_subtract_fusion
  (35 shorter events, 0.3 us)
Async XLA Ops:
  7.4 2.3 copy-start
  7.4 0.8 copy-start.10
  7.4 27.3 %reduce-scatter.10.cloned.1.call-start = ((), (), s32[]{:S(2)}) async-start(), calls=%async_computation.6 | async-start | bytes 143360
  10.4 1.9 copy-start.7
  11.5 0.6 copy-start.2
  12.2 81.8 %all-reduce.7.cloned.1.call-start = ((), (), s32[]{:S(2)}) async-start(), calls=%async_computation.3 | async-start | bytes 458752 | tf_op jit(solution)/shard_map/psum | solution.py:51
  19.9 1.1 copy-start.9
  21.2 0.7 copy-start.5
  22.0 101.0 %reduce-scatter.12.cloned.1.call-start = ((), (), s32[]{:S(2)}) async-start(), calls=%async_computation.7 | async-start | bytes 143360
  103.4 0.6 copy-start.3
  104.0 73.3 %all-reduce.9.cloned.1.call-start = ((), (), s32[]{:S(2)}) async-start(), calls=%async_computation.4 | async-start | bytes 458752 | tf_op jit(solution)/shard_map/psum | solution.py:51
  106.0 0.7 copy-start.6
  106.1 71.3 %copy-start.8 = (f32[448,128]{1,0:T(8,128)S(1)}, f32[448,128]{1,0:T(8,128)}, u32[]{:S(2)}) copy-start(f32[448,128]{1,0:T(8,128)} %all-reduce.7.cloned.1.call-done) | copy-start | bytes 688132
  106.8 99.5 %reduce-scatter.14.cloned.1.call-start = ((), (), s32[]{:S(2)}) async-start(), calls=%async_computation.8 | async-start | bytes 143360
  186.7 0.6 copy-start.1
  187.4 73.2 %all-reduce.11.cloned.1.call-start = ((), (), s32[]{:S(2)}) async-start(), calls=%async_computation.5 | async-start | bytes 458752 | tf_op jit(solution)/shard_map/psum | solution.py:51
  189.4 0.7 copy-start.4
Sparse Core Ops, SparseCore 0:
  12.3 22.2 reduce-scatter.9
  104.2 18.7 reduce-scatter.11
  187.5 18.7 reduce-scatter.13
Sparse Core Ops, SparseCore 1:
  22.0 71.9 all-reduce.6
  107.9 69.4 all-reduce.8
  191.2 69.3 all-reduce.10
where the time goes:
time: 270 us
  waiting for transfers between devices  120 us (44%)
  blocking collectives  110 us (41%)
  between operations  15.1 us (6%)
  other arithmetic  11.3 us (4%)
  local copies, waits for them, and re-layouts  8.42 us (3%)
  matrix products  4.35 us (2%)
    all_gather x3, blocking collectives, apply_operator(): return summed + lax.all_gather(mirror_own, 'col', axis=0, tiled=True)  93.2 us
    psum x3, waiting for transfers between devices, apply_operator(): summed = lax.psum(partial_sum, 'col')  74.8 us
    unnamed x9, waiting for transfers between devices  45.1 us
    all_gather x3, blocking collectives, apply_operator(): column_field = lax.all_gather(own_rows, 'row', axis=0, tiled=True)  17.2 us
  transfers between devices with their start and end apart: 6, of which 6 were waited for; matrix products, arithmetic and copies ran while one was open for 2% of the time, Pallas kernels for 0%

commit v1 on v0

v1 whole, which is shorter than its diff:
```python
import functools

import jax
import jax.numpy as jnp
from jax import lax
from jax.experimental import pallas as pl
from jax.experimental.pallas import tpu as pltpu
from jax.sharding import PartitionSpec as P

DEGREE = 3
MESH = pl.DeviceIdType.MESH

filter_low = 0.0
filter_high = 8.0


def halves(value):
    high = value.astype(jnp.bfloat16)
    return high, (value - high.astype(jnp.float32)).astype(jnp.bfloat16)


def product(left_high, left_low, right):
    right_high, right_low = halves(right)
    dot = functools.partial(jnp.dot, preferred_element_type=jnp.float32)
    return dot(left_high, right_high) + (dot(left_high, right_low) + dot(left_low, right_high))


def kernel(
    n_row, n_col, slot_ref, vectors_ref, tiles_ref, diag_ref, out_ref,
    dense, dense_h, dense_l, mirror_h, mirror_l,
    col_field, row_field, direct, mirror, direct_in, mirror_in, send_sem, recv_sem,
):
    orb = diag_ref.shape[0]
    rows, cols = n_col * orb, n_row * orb
    r, c = lax.axis_index("row"), lax.axis_index("col")
    row_peers = [lax.rem(r + d, n_row) for d in range(1, n_row)]
    col_peers = [lax.rem(c + d, n_col) for d in range(1, n_col)]

    def block(index):
        return pl.ds(pl.multiple_of(index * orb, 8), orb)

    barrier = pltpu.get_barrier_semaphore()
    for peer in row_peers:
        pl.semaphore_signal(barrier, inc=1, device_id=(peer, c), device_id_type=MESH)
    for peer in col_peers:
        pl.semaphore_signal(barrier, inc=1, device_id=(r, peer), device_id_type=MESH)

    def send(kind, step, source, target, device):
        pltpu.make_async_remote_copy(
            src_ref=source, dst_ref=target,
            send_sem=send_sem.at[kind, step], recv_sem=recv_sem.at[kind, step],
            device_id=device, device_id_type=MESH,
        ).start()

    def awaited(kind, step, region):
        return pltpu.make_async_remote_copy(
            src_ref=region, dst_ref=region,
            send_sem=send_sem.at[kind, step], recv_sem=recv_sem.at[kind, step],
            device_id=(r, c), device_id_type=MESH,
        )

    def region_of(kind, step):
        if kind == 0:
            return col_field.at[step, pl.ds(0, cols - orb)]
        if kind == 1:
            return direct_in.at[step]
        if kind == 2:
            return mirror_in.at[step]
        if step == DEGREE - 1:
            return out_ref.at[pl.ds(0, rows - orb)]
        return row_field.at[step, pl.ds(0, rows - orb)]

    pl.semaphore_wait(barrier, n_row + n_col - 2)

    own = vectors_ref[block(c), :]
    col_field[0, block(r), :] = own
    for peer in row_peers:
        send(0, 0, vectors_ref.at[block(c)], col_field.at[0, block(r)], (peer, c))

    dense[...] = jnp.zeros_like(dense)

    def fill(i, carry):
        parts = []
        for j in range(n_row):
            slot = slot_ref[i, j]
            tile = tiles_ref[jnp.maximum(slot - 1, 0)]
            parts.append(jnp.where(slot > 0, tile, 0.0))
        dense[block(i), pl.ds(0, cols)] = jnp.concatenate(parts, axis=1)
        return carry

    lax.fori_loop(0, n_col, fill, 0)
    whole = dense[...]
    dense_h[...], dense_l[...] = halves(whole)
    mirror_h[...], mirror_l[...] = halves(whole.T)
    diag_h, diag_l = halves(diag_ref[...])

    centre = 0.5 * (filter_high + filter_low)
    half_width = 0.5 * (filter_high - filter_low)
    previous = None
    for step in range(DEGREE):
        awaited(0, step, region_of(0, step)).wait_recv()
        direct[step] = product(
            dense_h[pl.ds(0, rows), pl.ds(0, cols)], dense_l[pl.ds(0, rows), pl.ds(0, cols)], col_field[step]
        )
        for d, peer in enumerate(col_peers):
            send(1, step, direct.at[step, block(peer)], direct_in.at[step, d], (r, peer))
        if step == 0:
            field = vectors_ref[...]
        else:
            awaited(3, step - 1, region_of(3, step - 1)).wait_recv()
            field = row_field[step - 1]
        mirror[step] = product(
            mirror_h[pl.ds(0, cols), pl.ds(0, rows)], mirror_l[pl.ds(0, cols), pl.ds(0, rows)], field
        )
        for d, peer in enumerate(row_peers):
            send(2, step, mirror.at[step, block(peer)], mirror_in.at[step, d], (peer, c))
        image = product(diag_h, diag_l, own) + direct[step, block(c), :] + mirror[step, block(r), :]
        awaited(2, step, region_of(2, step)).wait_recv()
        for d in range(n_row - 1):
            image = image + mirror_in[step, d]
        awaited(1, step, region_of(1, step)).wait_recv()
        for d in range(n_col - 1):
            image = image + direct_in[step, d]
        shifted = (image - centre * own) / half_width
        following = shifted if step == 0 else 2.0 * shifted - previous
        previous, own = own, following
        if step < DEGREE - 1:
            col_field[step + 1, block(r), :] = own
            row_field[step, block(c), :] = own
            for peer in row_peers:
                send(0, step + 1, row_field.at[step, block(c)], col_field.at[step + 1, block(r)], (peer, c))
            for peer in col_peers:
                send(3, step, row_field.at[step, block(c)], row_field.at[step, block(c)], (r, peer))
        else:
            out_ref[block(c), :] = own
            for peer in col_peers:
                send(3, step, out_ref.at[block(c)], out_ref.at[block(c)], (r, peer))
    awaited(3, DEGREE - 1, region_of(3, DEGREE - 1)).wait_recv()
    for kind in range(4):
        for step in range(DEGREE):
            awaited(kind, step, region_of(kind, step)).wait_send()


def up(value, unit):
    return (value + unit - 1) // unit * unit


def body(n_row, n_col, vectors, tiles, tile_pos, diag_blocks):
    tile_data = tiles[0, 0]
    stored, orb, _ = tile_data.shape
    width = vectors.shape[1]
    rows, cols = n_col * orb, n_row * orb
    at_row = tile_pos[0, 0, 0][:, None, None] == jnp.arange(n_col, dtype=jnp.int32)[None, :, None]
    at_col = tile_pos[0, 0, 1][:, None, None] == jnp.arange(n_row, dtype=jnp.int32)[None, None, :]
    number = jnp.arange(1, stored + 1, dtype=jnp.int32)[:, None, None]
    slots = jnp.sum(jnp.where(at_row & at_col, number, 0), axis=0)
    vmem = pl.BlockSpec(memory_space=pltpu.VMEM)
    f32, bf16 = jnp.float32, jnp.bfloat16
    tall, broad = up(rows, 128), up(cols, 128)
    return pl.pallas_call(
        functools.partial(kernel, n_row, n_col),
        out_shape=jax.ShapeDtypeStruct((rows, width), f32),
        in_specs=[pl.BlockSpec(memory_space=pltpu.SMEM), vmem, vmem, vmem],
        out_specs=vmem,
        scratch_shapes=[
            pltpu.VMEM((tall, broad), f32),
            pltpu.VMEM((tall, broad), bf16),
            pltpu.VMEM((tall, broad), bf16),
            pltpu.VMEM((broad, tall), bf16),
            pltpu.VMEM((broad, tall), bf16),
            pltpu.VMEM((DEGREE, cols, width), f32),
            pltpu.VMEM((DEGREE - 1, rows, width), f32),
            pltpu.VMEM((DEGREE, rows, width), f32),
            pltpu.VMEM((DEGREE, cols, width), f32),
            pltpu.VMEM((DEGREE, n_col - 1, orb, width), f32),
            pltpu.VMEM((DEGREE, n_row - 1, orb, width), f32),
            pltpu.SemaphoreType.DMA((4, DEGREE)),
            pltpu.SemaphoreType.DMA((4, DEGREE)),
        ],
        compiler_params=pltpu.CompilerParams(
            collective_id=0, has_side_effects=True, vmem_limit_bytes=48 * 1024 * 1024
        ),
        cost_estimate=pl.CostEstimate(
            flops=4 * DEGREE * rows * cols * width, bytes_accessed=8 * rows * width, transcendentals=0
        ),
    )(slots, vectors, tile_data, diag_blocks[0])


def solution(mesh):
    return jax.shard_map(
        functools.partial(body, mesh.shape["row"], mesh.shape["col"]),
        mesh=mesh,
        in_specs=(
            P("row", None),
            P("row", "col", None, None, None),
            P("row", "col", None, None),
            P(("row", "col"), None, None),
        ),
        out_specs=P("row", None),
        check_vma=False,
    )
```

time: 270 us -> 51.9 us (0.19)
  waiting for transfers between devices: 120 us -> 0 us
  blocking collectives: 110 us -> 0 us
  Pallas kernels: 0 us -> 47.3 us
  between operations: 15.1 us -> 0.02 us
  other arithmetic: 11.3 us -> 0.17 us
  matrix products: 4.35 us -> 0 us
  local copies, waits for them, and re-layouts: 8.42 us -> 4.1 us
    all_gather x6 -> x0, blocking collectives: 110 us -> none  [the longest x3 93.2 us: apply_operator(): return summed + lax.all_gather(mirror_own, 'col', axis=0, tiled=True)]
    psum x3 -> x0, waiting for transfers between devices: 74.8 us -> none  [apply_operator(): summed = lax.psum(partial_sum, 'col')]
    pallas_call x0 -> x1, Pallas kernels: none -> 47.3 us  [body(): pl.pallas_call(functools.partial(kernel, n_row, n_col), out_shape=jax.Sha...]
    unnamed x9 -> x0, waiting for transfers between devices: 45.1 us -> none
    scatter-add x6 -> x0, other arithmetic: 6.74 us -> none  [the longest x3 3.37 us: apply_operator(): jax.ops.segment_sum(mirror, block_cols, num_segments=column_blocks_n)]
    dot_general x9 -> x0, matrix products: 4.35 us -> none  [the longest x3 2 us: apply_operator(): jnp.einsum('tba,tbk->tak', tile_data, field_blocks[block_rows], precision...]
    gather x6 -> x0, local copies, waits for them, and re-layouts: 4.34 us -> none  [the longest x3 2.64 us: apply_operator(): field_blocks[block_rows]]
    sub x2 -> x0, other arithmetic: 2.72 us -> none  [body(): following = 2.0 * (image - centre * current) / half_width - previous]
  transfers between devices with their start and end apart: 6 -> 0, of which waited for: 6 -> 0; matrix products, arithmetic and copies ran while one was open for 2% -> 0% of each run, Pallas kernels for 0% -> 0%
where the time goes in v1:
time: 51.9 us; the launch traced here: 51.6 us
  Pallas kernels  47.3 us (91%)
  local copies, waits for them, and re-layouts  4.1 us (8%)
    pallas_call x1, Pallas kernels, body(): pl.pallas_call(functools.partial(kernel, n_row, n_col), out_shape=jax.Sha...  47.3 us
    unnamed x9, local copies, waits for them, and re-layouts  4.01 us

profile of v1, /device:TPU:0, one launch (start us, length us, event | category | flops | bytes accessed | tf_op | source)
XLA Modules:
  0.0 51.6 jit_solution(956938787552363483)
XLA Ops:
  0.0 0.0 copy-start.3
  0.0 0.7 %copy-done.3 = s32[1,1,2,10]{3,2,1,0:T(2,128)S(1)} copy-done((s32[1,1,2,10]{3,2,1,0:T(2,128)S(1)}, s32[1,1,2,10]{3,2,1,0:T(2,128)}, u32[]{:S(2)}) %copy-start.3) | copy-done | bytes 104
  0.7 0.1 select_reduce_fusion
  0.9 0.1 copy.5.slot_ref
  0.9 0.0 copy-start
  0.9 1.0 %copy-done = f32[1,1,10,56,56]{4,3,2,1,0:T(8,128)S(1)} copy-done((f32[1,1,10,56,56]{4,3,2,1,0:T(8,128)S(1)}, f32[1,1,10,56,56]{4,3,2,1,0:T(8,128)}, u32[]{:S(2)}) %copy-start) | copy-done | bytes 125464
  1.9 0.0 copy-start.1
  1.9 0.9 %copy-done.1 = f32[448,128]{1,0:T(8,128)S(1)} copy-done((f32[448,128]{1,0:T(8,128)S(1)}, f32[448,128]{1,0:T(8,128)}, u32[]{:S(2)}) %copy-start.1) | copy-done | bytes 229400
  2.8 0.0 copy-start.2
  2.8 0.7 %copy-done.2 = f32[1,56,56]{2,1,0:T(8,128)S(1)} copy-done((f32[1,56,56]{2,1,0:T(8,128)S(1)}, f32[1,56,56]{2,1,0:T(8,128)}, u32[]{:S(2)}) %copy-start.2) | copy-done | bytes 12568
  3.6 47.3 %shard_map.46 = f32[448,128]{1,0:T(8,128)S(1)} custom-call(s32[8,4]{1,0:T(8,128)S(1)} %copy.5.slot_ref, f32[448,128]{1,0:T(8,128)S(1)} %copy-done.1, f32[10,56,56]{2,1,0:T(8,128)S(1)} %bitcast.6, f32[56,56]{1,0:T(8,128)S(1)} %bitcast.7), custom_call_target="tpu_custom_call" | custom-call | flops 154140672 | bytes 458752 | tf_op jit(solution)/shard_map/pallas_call | solution.py:160
  50.9 0.7 %copy.7 = f32[448,128]{1,0:T(8,128)} copy(f32[448,128]{1,0:T(8,128)S(1)} %shard_map.46) | data formatting | bytes 458752
  (4 shorter events, 0.0 us)
Async XLA Ops:
  0.0 0.7 %copy-start.3 = (s32[1,1,2,10]{3,2,1,0:T(2,128)S(1)}, s32[1,1,2,10]{3,2,1,0:T(2,128)}, u32[]{:S(2)}) copy-start(s32[1,1,2,10]{3,2,1,0:T(2,128)} %param.6) | copy-start | bytes 244
  0.9 1.0 %copy-start = (f32[1,1,10,56,56]{4,3,2,1,0:T(8,128)S(1)}, f32[1,1,10,56,56]{4,3,2,1,0:T(8,128)}, u32[]{:S(2)}) copy-start(f32[1,1,10,56,56]{4,3,2,1,0:T(8,128)} %param.5) | copy-start | bytes 376324
  1.9 0.9 %copy-start.1 = (f32[448,128]{1,0:T(8,128)S(1)}, f32[448,128]{1,0:T(8,128)}, u32[]{:S(2)}) copy-start(f32[448,128]{1,0:T(8,128)} %vectors_ref.1) | copy-start | bytes 688132
  2.8 0.7 %copy-start.2 = (f32[1,56,56]{2,1,0:T(8,128)S(1)}, f32[1,56,56]{2,1,0:T(8,128)}, u32[]{:S(2)}) copy-start(f32[1,56,56]{2,1,0:T(8,128)} %param.7) | copy-start | bytes 37636

commit v2 on v1

v2 whole, which is shorter than its diff:
```python
import functools

import jax
import jax.numpy as jnp
from jax import lax
from jax.experimental import pallas as pl
from jax.experimental.pallas import tpu as pltpu
from jax.sharding import PartitionSpec as P

DEGREE = 3
MESH = pl.DeviceIdType.MESH

filter_low = 0.0
filter_high = 8.0


def halves(value):
    high = value.astype(jnp.bfloat16)
    return high, (value - high.astype(jnp.float32)).astype(jnp.bfloat16)


def product(left_high, left_low, right):
    right_high, right_low = halves(right)
    dot = functools.partial(jnp.dot, preferred_element_type=jnp.float32)
    return dot(left_high, right_high) + (dot(left_high, right_low) + dot(left_low, right_high))


def mix(fixed, rolled, field, left):
    far = pltpu.roll(field, field.shape[1] // 2, 1)
    both = product(fixed[0][...], fixed[1][...], field) + product(rolled[0][...], rolled[1][...], far)
    count = both.shape[0] // 2
    return jnp.where(left, both[:count], both[count:])


def kernel(
    n_row, n_col, slot_hbm, vectors_hbm, tiles_hbm, diag_hbm, out_ref,
    slots, slots_smem, vectors, tiles, diags, packed, dense,
    down_fixed_h, down_fixed_l, down_rolled_h, down_rolled_l,
    up_fixed_h, up_fixed_l, up_rolled_h, up_rolled_l,
    col_field, row_field, final, direct, mirror, direct_in, mirror_in,
    load_sem, send_sem, recv_sem,
):
    orb = diag_hbm.shape[0]
    width = vectors.shape[1]
    stored = tiles.shape[1]
    half = n_col // 2
    rows, cols = half * orb, n_row * orb
    r, c = lax.axis_index("row"), lax.axis_index("col")
    h, m = c // half, c % half
    other = 1 - h
    partner = other * half + m
    row_peers = [lax.rem(r + d, n_row) for d in range(1, n_row)]
    col_slots = [lax.rem(m + d, half) for d in range(1, half)]
    left = lax.broadcasted_iota(jnp.int32, (1, width), 1) < width // 2

    def block(index):
        return pl.ds(pl.multiple_of(index * orb, 8), orb)

    loads = [
        pltpu.make_async_copy(slot_hbm, slots.at[0], load_sem.at[0]),
        pltpu.make_async_copy(vectors_hbm, vectors, load_sem.at[1]),
        pltpu.make_async_copy(tiles_hbm, tiles.at[0], load_sem.at[2]),
        pltpu.make_async_copy(diag_hbm, diags.at[0], load_sem.at[3]),
        pltpu.make_async_copy(slot_hbm, slots_smem.at[0], load_sem.at[4]),
    ]
    for load in loads:
        load.start()

    barrier = pltpu.get_barrier_semaphore()
    for peer in row_peers:
        pl.semaphore_signal(barrier, inc=1, device_id=(peer, c), device_id_type=MESH)
    for slot in col_slots:
        pl.semaphore_signal(barrier, inc=1, device_id=(r, h * half + slot), device_id_type=MESH)
    pl.semaphore_signal(barrier, inc=1, device_id=(r, partner), device_id_type=MESH)

    def copy(kind, step, source, target, device):
        return pltpu.make_async_remote_copy(
            src_ref=source, dst_ref=target,
            send_sem=send_sem.at[kind, step], recv_sem=recv_sem.at[kind, step],
            device_id=device, device_id_type=MESH,
        )

    def region_of(kind, step):
        if kind == 0:
            return col_field.at[step, pl.ds(0, cols - orb)]
        if kind == 1:
            return direct_in.at[step]
        if kind == 2:
            return mirror_in.at[step]
        if kind == 3 and step < DEGREE - 1:
            return row_field.at[step, pl.ds(0, rows - orb)]
        if kind == 3 or step == 3:
            return final.at[0, pl.ds(0, rows - orb)]
        if step == 0:
            return packed.at[1]
        if step == 1:
            return slots.at[1]
        return final.at[0, pl.ds(0, orb)]

    def awaited(kind, step):
        region = region_of(kind, step)
        return copy(kind, step, region, region, (r, c))

    loads[2].wait()
    loads[3].wait()
    part = (width - 2 * orb) // 8 * 8
    for k in range(stored // 2):
        pieces = [tiles[0, 2 * k], tiles[0, 2 * k + 1]]
        if k * part < orb:
            share = min(part, orb - k * part)
            pieces.append(diags[0, :, pl.ds(k * part, share)])
            if share < part:
                pieces.append(jnp.zeros((orb, part - share), jnp.float32))
        else:
            pieces.append(jnp.zeros((orb, part), jnp.float32))
        packed[0, k] = jnp.concatenate(pieces, axis=1)
    loads[0].wait()
    loads[1].wait()
    top, bottom = vectors[pl.ds(0, rows), :], vectors[pl.ds(rows, rows), :]
    first = jnp.where(h == 0, top, pltpu.roll(top, width // 2, 1))
    second = jnp.where(h == 0, pltpu.roll(bottom, width // 2, 1), bottom)
    row_field[DEGREE - 1] = jnp.where(left, first, second)
    own = row_field[DEGREE - 1, block(m), :]
    col_field[0, block(r), :] = own

    pl.semaphore_wait(barrier, n_row + half - 1)

    copy(4, 1, slots.at[0], slots.at[1], (r, partner)).start()
    copy(4, 0, packed.at[0], packed.at[1], (r, partner)).start()
    for peer in row_peers:
        copy(0, 0, row_field.at[DEGREE - 1, block(m)], col_field.at[0, block(r)], (peer, c)).start()

    dense[...] = jnp.zeros_like(dense)
    loads[4].wait()

    def fill(source, place):
        for a in range(2):
            def one(i, carry):
                parts = []
                for j in range(n_row):
                    slot = slots_smem[source, a * half + i, j]
                    tile = tiles[source, jnp.maximum(slot - 1, 0)]
                    parts.append(jnp.where(slot > 0, tile, 0.0))
                dense[a, place, block(i), pl.ds(0, cols)] = jnp.concatenate(parts, axis=1)
                return carry

            lax.fori_loop(0, half, one, 0)

    fill(0, h)
    awaited(4, 1).wait_recv()
    other_slots = pltpu.make_async_copy(slots.at[1], slots_smem.at[1], load_sem.at[5])
    other_slots.start()
    other_slots.wait()
    awaited(4, 0).wait_recv()
    pieces = []
    for k in range(stored // 2):
        pair = packed[1, k]
        tiles[1, 2 * k] = pair[:, :orb]
        tiles[1, 2 * k + 1] = pair[:, orb : 2 * orb]
        if k * part < orb:
            pieces.append(pair[:, 2 * orb : 2 * orb + min(part, orb - k * part)])
    diags[1] = jnp.concatenate(pieces, axis=1)
    fill(1, other)

    near, far = pl.ds(0, rows), pl.ds(rows, rows)
    for target_h, target_l, parts in (
        (down_fixed_h, down_fixed_l, ((0, 0), (1, 1))), (down_rolled_h, down_rolled_l, ((0, 1), (1, 0))),
    ):
        for place, (a, b) in zip((near, far), parts):
            target_h[place, :], target_l[place, :] = halves(dense[a, b, pl.ds(0, rows), pl.ds(0, cols)])
    near, far = pl.ds(0, cols), pl.ds(cols, cols)
    for target_h, target_l, parts in (
        (up_fixed_h, up_fixed_l, ((0, 0), (1, 1))), (up_rolled_h, up_rolled_l, ((1, 0), (0, 1))),
    ):
        for place, (a, b) in zip((near, far), parts):
            target_h[place, :], target_l[place, :] = halves(dense[a, b].T[:cols, :rows])
    diag_left = halves(jnp.where(h == 0, diags[0], diags[1]))
    diag_right = halves(jnp.where(h == 0, diags[1], diags[0]))

    centre = 0.5 * (filter_high + filter_low)
    half_width = 0.5 * (filter_high - filter_low)
    previous = None
    for step in range(DEGREE):
        awaited(0, step).wait_recv()
        direct[step] = mix((down_fixed_h, down_fixed_l), (down_rolled_h, down_rolled_l), col_field[step], left)
        for d, slot in enumerate(col_slots):
            copy(1, step, direct.at[step, block(slot)], direct_in.at[step, d], (r, h * half + slot)).start()
        if step == 0:
            field = row_field[DEGREE - 1]
        else:
            awaited(3, step - 1).wait_recv()
            field = row_field[step - 1]
        mirror[step] = mix((up_fixed_h, up_fixed_l), (up_rolled_h, up_rolled_l), field, left)
        for d, peer in enumerate(row_peers):
            copy(2, step, mirror.at[step, block(peer)], mirror_in.at[step, d], (peer, c)).start()
        image = jnp.where(left, product(*diag_left, own), product(*diag_right, own))
        image = image + direct[step, block(m), :] + mirror[step, block(r), :]
        awaited(1, step).wait_recv()
        for d in range(half - 1):
            image = image + direct_in[step, d]
        awaited(2, step).wait_recv()
        for d in range(n_row - 1):
            image = image + mirror_in[step, d]
        shifted = (image - centre * own) / half_width
        following = shifted if step == 0 else 2.0 * shifted - previous
        previous, own = own, following
        if step < DEGREE - 1:
            col_field[step + 1, block(r), :] = own
            row_field[step, block(m), :] = own
            mine = row_field.at[step, block(m)]
            for peer in row_peers:
                copy(0, step + 1, mine, col_field.at[step + 1, block(r)], (peer, c)).start()
            for slot in col_slots:
                copy(3, step, mine, mine, (r, h * half + slot)).start()
    final[h, block(m), :] = own
    mine, theirs = final.at[h, block(m)], final.at[other, block(m)]
    copy(4, 2, mine, mine, (r, partner)).start()
    for slot in col_slots:
        copy(3, DEGREE - 1, mine, mine, (r, h * half + slot)).start()
    awaited(4, 2).wait_recv()
    for slot in col_slots:
        copy(4, 3, theirs, theirs, (r, h * half + slot)).start()
    awaited(3, DEGREE - 1).wait_recv()
    awaited(4, 3).wait_recv()
    low, high = final[0], final[1]
    out_ref[pl.ds(0, rows), :] = jnp.where(left, low, pltpu.roll(high, width // 2, 1))
    out_ref[pl.ds(rows, rows), :] = jnp.where(left, pltpu.roll(low, width // 2, 1), high)
    for kind in range(5):
        for step in range(4 if kind == 4 else DEGREE):
            awaited(kind, step).wait_send()


def up(value, unit):
    return (value + unit - 1) // unit * unit


def body(n_row, n_col, vectors, tiles, tile_pos, diag_blocks):
    tile_data = tiles[0, 0]
    stored, orb, _ = tile_data.shape
    width = vectors.shape[1]
    half = n_col // 2
    rows, cols = half * orb, n_row * orb
    at_row = tile_pos[0, 0, 0][:, None, None] == jnp.arange(n_col, dtype=jnp.int32)[None, :, None]
    at_col = tile_pos[0, 0, 1][:, None, None] == jnp.arange(128, dtype=jnp.int32)[None, None, :]
    number = jnp.arange(1, stored + 1, dtype=jnp.int32)[:, None, None]
    slots = jnp.sum(jnp.where(at_row & at_col, number, 0), axis=0)
    hbm = pl.BlockSpec(memory_space=pl.ANY)
    f32, bf16, i32 = jnp.float32, jnp.bfloat16, jnp.int32
    down = pltpu.VMEM((2 * rows, cols), bf16)
    upward = pltpu.VMEM((2 * cols, rows), bf16)
    return pl.pallas_call(
        functools.partial(kernel, n_row, n_col),
        out_shape=jax.ShapeDtypeStruct((2 * rows, width), f32),
        in_specs=[hbm, hbm, hbm, hbm],
        out_specs=pl.BlockSpec(memory_space=pltpu.VMEM),
        scratch_shapes=[
            pltpu.VMEM((2, n_col, 128), i32),
            pltpu.SMEM((2, n_col, 128), i32),
            pltpu.VMEM((2 * rows, width), f32),
            pltpu.VMEM((2, stored, orb, orb), f32),
            pltpu.VMEM((2, orb, orb), f32),
            pltpu.VMEM((2, stored // 2, orb, width), f32),
            pltpu.VMEM((2, 2, up(rows, 128), up(cols, 128)), f32),
            down, down, down, down, upward, upward, upward, upward,
            pltpu.VMEM((DEGREE, cols, width), f32),
            pltpu.VMEM((DEGREE, rows, width), f32),
            pltpu.VMEM((2, rows, width), f32),
            pltpu.VMEM((DEGREE, rows, width), f32),
            pltpu.VMEM((DEGREE, cols, width), f32),
            pltpu.VMEM((DEGREE, half - 1, orb, width), f32),
            pltpu.VMEM((DEGREE, n_row - 1, orb, width), f32),
            pltpu.SemaphoreType.DMA((6,)),
            pltpu.SemaphoreType.DMA((5, 4)),
            pltpu.SemaphoreType.DMA((5, 4)),
        ],
        compiler_params=pltpu.CompilerParams(
            collective_id=0, has_side_effects=True, vmem_limit_bytes=56 * 1024 * 1024
        ),
        cost_estimate=pl.CostEstimate(
            flops=16 * DEGREE * rows * cols * width, bytes_accessed=8 * rows * width, transcendentals=0
        ),
    )(slots, vectors, tile_data, diag_blocks[0])


def solution(mesh):
    return jax.shard_map(
        functools.partial(body, mesh.shape["row"], mesh.shape["col"]),
        mesh=mesh,
        in_specs=(
            P("row", None),
            P("row", "col", None, None, None),
            P("row", "col", None, None),
            P(("row", "col"), None, None),
        ),
        out_specs=P("row", None),
        check_vma=False,
    )
```

time: 51.9 us -> 46.7 us (0.90)
  Pallas kernels: 47.3 us -> 43.4 us
  local copies, waits for them, and re-layouts: 4.1 us -> 2.32 us
  other arithmetic: 0.17 us -> 0.84 us
    pallas_call x1, Pallas kernels: 47.3 us -> 43.4 us  [body(): pl.pallas_call(functools.partial(kernel, n_row, n_col), out_shape=jax.Sha...]
    unnamed x9 -> x3, local copies, waits for them, and re-layouts: 4.01 us -> 2.32 us
    reduce_sum x1, other arithmetic: 0.15 us -> 0.69 us  [body(): slots = jnp.sum(jnp.where(at_row & at_col, number, 0), axis=0)]
where the time goes in v2:
time: 46.7 us; the launch traced here: 46.5 us
  Pallas kernels  43.4 us (93%)
  local copies, waits for them, and re-layouts  2.32 us (5%)
  other arithmetic  0.84 us (2%)
    pallas_call x1, Pallas kernels, body(): pl.pallas_call(functools.partial(kernel, n_row, n_col), out_shape=jax.Sha...  43.4 us
    unnamed x3, local copies, waits for them, and re-layouts  2.32 us

profile of v2, /device:TPU:0, one launch (start us, length us, event | category | flops | bytes accessed | tf_op | source)
XLA Modules:
  0.0 46.5 jit_solution(850506841268746032)
XLA Ops:
  0.0 0.0 copy-start
  0.0 0.7 %copy-done = s32[1,1,2,10]{3,2,1,0:T(2,128)S(1)} copy-done((s32[1,1,2,10]{3,2,1,0:T(2,128)S(1)}, s32[1,1,2,10]{3,2,1,0:T(2,128)}, u32[]{:S(2)}) %copy-start) | copy-done | bytes 104
  0.7 0.1 iota_compare_fusion.1
  0.8 0.1 iota_compare_fusion
  0.8 0.7 %select_reduce_fusion.slot_hbm = s32[8,128]{1,0:T(8,128)} fusion(s32[10]{0:T(128)S(1)} %iota_add_fusion, pred[10,128]{1,0:T(8,128)(4,1)S(1)} %iota_compare_fusion, pred[10,8]{1,0:T(8,128)(4,1)S(1)} %iota_compare_fusion.1), kind=kLoop, calls=%fused_computation | loop fusion | flops 29696 | bytes 5496 | tf_op jit(solution)/shard_map/reduce_sum | solution.py:246
  1.5 43.4 %shard_map.46 = f32[448,128]{1,0:T(8,128)} custom-call(s32[8,128]{1,0:T(8,128)} %select_reduce_fusion.slot_hbm, f32[448,128]{1,0:T(8,128)} %vectors_hbm.1, f32[10,56,56]{2,1,0:T(8,128)} %bitcast.6, f32[56,56]{1,0:T(8,128)} %bitcast.7), custom_call_target="tpu_custom_call" | custom-call | flops 308281344 | bytes 229376 | tf_op jit(solution)/shard_map/pallas_call | solution.py:251
  44.9 1.6 %copy.6 = f32[448,128]{1,0:T(8,128)} copy(f32[448,128]{1,0:T(8,128)} %shard_map.46) | data formatting | bytes 458752
  (2 shorter events, 0.0 us)
Async XLA Ops:
  0.0 0.7 %copy-start = (s32[1,1,2,10]{3,2,1,0:T(2,128)S(1)}, s32[1,1,2,10]{3,2,1,0:T(2,128)}, u32[]{:S(2)}) copy-start(s32[1,1,2,10]{3,2,1,0:T(2,128)} %param.6) | copy-start | bytes 244

commit v3 on v2

--- a/solution.py
+++ b/solution.py
@@ -25,18 +25,17 @@
     return dot(left_high, right_high) + (dot(left_high, right_low) + dot(left_low, right_high))
 
 
-def mix(fixed, rolled, field, left):
+def mix(high, low, field, left):
     far = pltpu.roll(field, field.shape[1] // 2, 1)
-    both = product(fixed[0][...], fixed[1][...], field) + product(rolled[0][...], rolled[1][...], far)
+    both = product(high[0], low[0], field) + product(high[1], low[1], far)
     count = both.shape[0] // 2
     return jnp.where(left, both[:count], both[count:])
 
 
 def kernel(
-    n_row, n_col, slot_hbm, vectors_hbm, tiles_hbm, diag_hbm, out_ref,
-    slots, slots_smem, vectors, tiles, diags, packed, dense,
-    down_fixed_h, down_fixed_l, down_rolled_h, down_rolled_l,
-    up_fixed_h, up_fixed_l, up_rolled_h, up_rolled_l,
+    n_row, n_col, pos_hbm, vectors_hbm, tiles_hbm, diag_hbm, out_ref,
+    pos, slots, slots_smem, vectors, tiles, diags, packed, dense,
+    down_h, down_l, up_h, up_l,
     col_field, row_field, final, direct, mirror, direct_in, mirror_in,
     load_sem, send_sem, recv_sem,
 ):
@@ -57,11 +56,10 @@
         return pl.ds(pl.multiple_of(index * orb, 8), orb)
 
     loads = [
-        pltpu.make_async_copy(slot_hbm, slots.at[0], load_sem.at[0]),
+        pltpu.make_async_copy(pos_hbm, pos, load_sem.at[0]),
         pltpu.make_async_copy(vectors_hbm, vectors, load_sem.at[1]),
         pltpu.make_async_copy(tiles_hbm, tiles.at[0], load_sem.at[2]),
         pltpu.make_async_copy(diag_hbm, diags.at[0], load_sem.at[3]),
-        pltpu.make_async_copy(slot_hbm, slots_smem.at[0], load_sem.at[4]),
     ]
     for load in loads:
         load.start()
@@ -87,9 +85,9 @@
             return direct_in.at[step]
         if kind == 2:
             return mirror_in.at[step]
-        if kind == 3 and step < DEGREE - 1:
+        if kind == 3:
             return row_field.at[step, pl.ds(0, rows - orb)]
-        if kind == 3 or step == 3:
+        if step == 3:
             return final.at[0, pl.ds(0, rows - orb)]
         if step == 0:
             return packed.at[1]
@@ -115,12 +113,20 @@
             pieces.append(jnp.zeros((orb, part), jnp.float32))
         packed[0, k] = jnp.concatenate(pieces, axis=1)
     loads[0].wait()
+    at_row = lax.broadcasted_iota(jnp.int32, (n_col, 128), 0)
+    at_col = lax.broadcasted_iota(jnp.int32, (n_col, 128), 1)
+    table = jnp.zeros((n_col, 128), jnp.int32)
+    for t in range(stored):
+        table = jnp.where((at_row == pos[0, t]) & (at_col == pos[1, t]), t + 1, table)
+    slots[0] = table
+    own_slots = pltpu.make_async_copy(slots.at[0], slots_smem.at[0], load_sem.at[4])
+    own_slots.start()
     loads[1].wait()
     top, bottom = vectors[pl.ds(0, rows), :], vectors[pl.ds(rows, rows), :]
     first = jnp.where(h == 0, top, pltpu.roll(top, width // 2, 1))
     second = jnp.where(h == 0, pltpu.roll(bottom, width // 2, 1), bottom)
-    row_field[DEGREE - 1] = jnp.where(left, first, second)
-    own = row_field[DEGREE - 1, block(m), :]
+    row_field[0] = jnp.where(left, first, second)
+    own = row_field[0, block(m), :]
     col_field[0, block(r), :] = own
 
     pl.semaphore_wait(barrier, n_row + half - 1)
@@ -128,10 +134,10 @@
     copy(4, 1, slots.at[0], slots.at[1], (r, partner)).start()
     copy(4, 0, packed.at[0], packed.at[1], (r, partner)).start()
     for peer in row_peers:
-        copy(0, 0, row_field.at[DEGREE - 1, block(m)], col_field.at[0, block(r)], (peer, c)).start()
+        copy(0, 0, row_field.at[0, block(m)], col_field.at[0, block(r)], (peer, c)).start()
 
     dense[...] = jnp.zeros_like(dense)
-    loads[4].wait()
+    own_slots.wait()
 
     def fill(source, place):
         for a in range(2):
@@ -141,10 +147,16 @@
                     slot = slots_smem[source, a * half + i, j]
                     tile = tiles[source, jnp.maximum(slot - 1, 0)]
                     parts.append(jnp.where(slot > 0, tile, 0.0))
-                dense[a, place, block(i), pl.ds(0, cols)] = jnp.concatenate(parts, axis=1)
+                dense[a, block(i), pl.ds(0, cols)] = jnp.concatenate(parts, axis=1)
                 return carry
 
             lax.fori_loop(0, half, one, 0)
+            turned = place if a == 0 else 1 - place
+            panel = dense[a]
+            there = pl.ds(a * rows, rows)
+            down_h[turned, there, :], down_l[turned, there, :] = halves(panel[:rows, :cols])
+            there = pl.ds(pl.multiple_of(place * cols, 16), cols)
+            up_h[turned, there, :], up_l[turned, there, :] = halves(panel.T[:cols, :rows])
 
     fill(0, h)
     awaited(4, 1).wait_recv()
@@ -162,35 +174,24 @@
     diags[1] = jnp.concatenate(pieces, axis=1)
     fill(1, other)
 
-    near, far = pl.ds(0, rows), pl.ds(rows, rows)
-    for target_h, target_l, parts in (
-        (down_fixed_h, down_fixed_l, ((0, 0), (1, 1))), (down_rolled_h, down_rolled_l, ((0, 1), (1, 0))),
-    ):
-        for place, (a, b) in zip((near, far), parts):
-            target_h[place, :], target_l[place, :] = halves(dense[a, b, pl.ds(0, rows), pl.ds(0, cols)])
-    near, far = pl.ds(0, cols), pl.ds(cols, cols)
-    for target_h, target_l, parts in (
-        (up_fixed_h, up_fixed_l, ((0, 0), (1, 1))), (up_rolled_h, up_rolled_l, ((1, 0), (0, 1))),
-    ):
-        for place, (a, b) in zip((near, far), parts):
-            target_h[place, :], target_l[place, :] = halves(dense[a, b].T[:cols, :rows])
     diag_left = halves(jnp.where(h == 0, diags[0], diags[1]))
     diag_right = halves(jnp.where(h == 0, diags[1], diags[0]))
 
     centre = 0.5 * (filter_high + filter_low)
     half_width = 0.5 * (filter_high - filter_low)
-    previous = None
-    for step in range(DEGREE):
+
+    def one_step(step, carry):
+        previous, own = carry
         awaited(0, step).wait_recv()
-        direct[step] = mix((down_fixed_h, down_fixed_l), (down_rolled_h, down_rolled_l), col_field[step], left)
+        direct[step] = mix(down_h, down_l, col_field[step], left)
         for d, slot in enumerate(col_slots):
             copy(1, step, direct.at[step, block(slot)], direct_in.at[step, d], (r, h * half + slot)).start()
-        if step == 0:
-            field = row_field[DEGREE - 1]
-        else:
-            awaited(3, step - 1).wait_recv()
-            field = row_field[step - 1]
-        mirror[step] = mix((up_fixed_h, up_fixed_l), (up_rolled_h, up_rolled_l), field, left)
+
+        @pl.when(step > 0)
+        def _():
+            awaited(3, step).wait_recv()
+
+        mirror[step] = mix(up_h, up_l, row_field[step], left)
         for d, peer in enumerate(row_peers):
             copy(2, step, mirror.at[step, block(peer)], mirror_in.at[step, d], (peer, c)).start()
         image = jnp.where(left, product(*diag_left, own), product(*diag_right, own))
@@ -202,25 +203,30 @@
         for d in range(n_row - 1):
             image = image + mirror_in[step, d]
         shifted = (image - centre * own) / half_width
-        following = shifted if step == 0 else 2.0 * shifted - previous
-        previous, own = own, following
-        if step < DEGREE - 1:
-            col_field[step + 1, block(r), :] = own
-            row_field[step, block(m), :] = own
-            mine = row_field.at[step, block(m)]
+        following = jnp.where(step == 0, shifted, 2.0 * shifted - previous)
+
+        @pl.when(step < DEGREE - 1)
+        def _():
+            row_field[step + 1, block(m), :] = following
+            col_field[step + 1, block(r), :] = following
+            mine = row_field.at[step + 1, block(m)]
             for peer in row_peers:
                 copy(0, step + 1, mine, col_field.at[step + 1, block(r)], (peer, c)).start()
             for slot in col_slots:
-                copy(3, step, mine, mine, (r, h * half + slot)).start()
+                copy(3, step + 1, mine, mine, (r, h * half + slot)).start()
+
+        return own, following
+
+    _, own = lax.fori_loop(0, DEGREE, one_step, (jnp.zeros_like(own), own))
     final[h, block(m), :] = own
     mine, theirs = final.at[h, block(m)], final.at[other, block(m)]
     copy(4, 2, mine, mine, (r, partner)).start()
     for slot in col_slots:
-        copy(3, DEGREE - 1, mine, mine, (r, h * half + slot)).start()
+        copy(3, 0, mine, mine, (r, h * half + slot)).start()
     awaited(4, 2).wait_recv()
     for slot in col_slots:
         copy(4, 3, theirs, theirs, (r, h * half + slot)).start()
-    awaited(3, DEGREE - 1).wait_recv()
+    awaited(3, 0).wait_recv()
     awaited(4, 3).wait_recv()
     low, high = final[0], final[1]
     out_ref[pl.ds(0, rows), :] = jnp.where(left, low, pltpu.roll(high, width // 2, 1))
@@ -240,28 +246,25 @@
     width = vectors.shape[1]
     half = n_col // 2
     rows, cols = half * orb, n_row * orb
-    at_row = tile_pos[0, 0, 0][:, None, None] == jnp.arange(n_col, dtype=jnp.int32)[None, :, None]
-    at_col = tile_pos[0, 0, 1][:, None, None] == jnp.arange(128, dtype=jnp.int32)[None, None, :]
-    number = jnp.arange(1, stored + 1, dtype=jnp.int32)[:, None, None]
-    slots = jnp.sum(jnp.where(at_row & at_col, number, 0), axis=0)
     hbm = pl.BlockSpec(memory_space=pl.ANY)
     f32, bf16, i32 = jnp.float32, jnp.bfloat16, jnp.int32
-    down = pltpu.VMEM((2 * rows, cols), bf16)
-    upward = pltpu.VMEM((2 * cols, rows), bf16)
+    down = pltpu.VMEM((2, 2 * rows, cols), bf16)
+    upward = pltpu.VMEM((2, 2 * cols, rows), bf16)
     return pl.pallas_call(
         functools.partial(kernel, n_row, n_col),
         out_shape=jax.ShapeDtypeStruct((2 * rows, width), f32),
         in_specs=[hbm, hbm, hbm, hbm],
         out_specs=pl.BlockSpec(memory_space=pltpu.VMEM),
         scratch_shapes=[
+            pltpu.SMEM(tile_pos.shape[2:], i32),
             pltpu.VMEM((2, n_col, 128), i32),
             pltpu.SMEM((2, n_col, 128), i32),
             pltpu.VMEM((2 * rows, width), f32),
             pltpu.VMEM((2, stored, orb, orb), f32),
             pltpu.VMEM((2, orb, orb), f32),
             pltpu.VMEM((2, stored // 2, orb, width), f32),
-            pltpu.VMEM((2, 2, up(rows, 128), up(cols, 128)), f32),
-            down, down, down, down, upward, upward, upward, upward,
+            pltpu.VMEM((2, up(rows, 128), up(cols, 128)), f32),
+            down, down, upward, upward,
             pltpu.VMEM((DEGREE, cols, width), f32),
             pltpu.VMEM((DEGREE, rows, width), f32),
             pltpu.VMEM((2, rows, width), f32),
@@ -279,7 +282,7 @@
         cost_estimate=pl.CostEstimate(
             flops=16 * DEGREE * rows * cols * width, bytes_accessed=8 * rows * width, transcendentals=0
         ),
-    )(slots, vectors, tile_data, diag_blocks[0])
+    )(tile_pos[0, 0], vectors, tile_data, diag_blocks[0])
 
 
 def solution(mesh):

time: 46.7 us -> 45 us (0.964)
  other arithmetic: 0.84 us -> 0 us
  local copies, waits for them, and re-layouts: 2.32 us -> 1.64 us
    reduce_sum x1 -> x0, other arithmetic: 0.69 us -> none  [body(): slots = jnp.sum(jnp.where(at_row & at_col, number, 0), axis=0)]
    unnamed x3 -> x1, local copies, waits for them, and re-layouts: 2.32 us -> 1.64 us
where the time goes in v3:
time: 45 us; the launch traced here: 44.9 us
  Pallas kernels  43.2 us (96%)
  local copies, waits for them, and re-layouts  1.64 us (4%)
    pallas_call x1, Pallas kernels, body(): pl.pallas_call(functools.partial(kernel, n_row, n_col), out_shape=jax.Sha...  43.2 us
    unnamed x1, local copies, waits for them, and re-layouts  1.64 us

profile of v3, /device:TPU:0, one launch (start us, length us, event | category | flops | bytes accessed | tf_op | source)
XLA Modules:
  0.0 44.9 jit_solution(16479347539165391357)
XLA Ops:
  0.0 43.2 %shard_map.46 = f32[448,128]{1,0:T(8,128)} custom-call(s32[2,10]{1,0:T(2,128)} %bitcast.5, f32[448,128]{1,0:T(8,128)} %vectors_hbm.1, f32[10,56,56]{2,1,0:T(8,128)} %bitcast.3, f32[56,56]{1,0:T(8,128)} %bitcast.4), custom_call_target="tpu_custom_call" | custom-call | flops 308281344 | bytes 229376 | tf_op jit(solution)/shard_map/pallas_call | solution.py:253
  43.2 1.6 %copy.6 = f32[448,128]{1,0:T(8,128)} copy(f32[448,128]{1,0:T(8,128)} %shard_map.46) | data formatting | bytes 458752

commit v4 on v3

--- a/solution.py
+++ b/solution.py
@@ -25,9 +25,14 @@
     return dot(left_high, right_high) + (dot(left_high, right_low) + dot(left_low, right_high))
 
 
-def mix(high, low, field, left):
+def mix(panels, field, left):
     far = pltpu.roll(field, field.shape[1] // 2, 1)
-    both = product(high[0], low[0], field) + product(high[1], low[1], far)
+    depth = panels.shape[1] // 4
+    empty = jnp.zeros((depth - field.shape[0], field.shape[1]), jnp.float32)
+    pieces = [field, far] if depth == field.shape[0] else [field, empty, far, empty]
+    high, low = halves(jnp.concatenate(pieces, axis=0))
+    dot = functools.partial(jnp.dot, preferred_element_type=jnp.float32)
+    both = dot(panels[...], jnp.concatenate([high, high], axis=0)) + dot(panels[:, pl.ds(0, 2 * depth)], low)
     count = both.shape[0] // 2
     return jnp.where(left, both[:count], both[count:])
 
@@ -35,7 +40,7 @@
 def kernel(
     n_row, n_col, pos_hbm, vectors_hbm, tiles_hbm, diag_hbm, out_ref,
     pos, slots, slots_smem, vectors, tiles, diags, packed, dense,
-    down_h, down_l, up_h, up_l,
+    down, upward,
     col_field, row_field, final, direct, mirror, direct_in, mirror_in,
     load_sem, send_sem, recv_sem,
 ):
@@ -151,14 +156,21 @@
                 return carry
 
             lax.fori_loop(0, half, one, 0)
-            turned = place if a == 0 else 1 - place
-            panel = dense[a]
-            there = pl.ds(a * rows, rows)
-            down_h[turned, there, :], down_l[turned, there, :] = halves(panel[:rows, :cols])
-            there = pl.ds(pl.multiple_of(place * cols, 16), cols)
-            up_h[turned, there, :], up_l[turned, there, :] = halves(panel.T[:cols, :rows])
+            put(down, place if a == 0 else 1 - place, pl.ds(a * rows, rows), dense[a, pl.ds(0, rows), :])
+
+    def put(panels, turned, there, panel):
+        depth = panel.shape[1]
+        high, low = halves(panel)
+        panels[there, pl.ds(pl.multiple_of(turned * depth, 128), depth)] = high
+        panels[there, pl.ds(pl.multiple_of((turned + 2) * depth, 128), depth)] = low
+
+    def turn(place):
+        there = pl.ds(pl.multiple_of(place * cols, 16), cols)
+        for a in range(2):
+            put(upward, place if a == 0 else 1 - place, there, dense[a].T[:cols])
 
     fill(0, h)
+    turn(h)
     awaited(4, 1).wait_recv()
     other_slots = pltpu.make_async_copy(slots.at[1], slots_smem.at[1], load_sem.at[5])
     other_slots.start()
@@ -183,15 +195,19 @@
     def one_step(step, carry):
         previous, own = carry
         awaited(0, step).wait_recv()
-        direct[step] = mix(down_h, down_l, col_field[step], left)
+        direct[step] = mix(down, col_field[step], left)
         for d, slot in enumerate(col_slots):
             copy(1, step, direct.at[step, block(slot)], direct_in.at[step, d], (r, h * half + slot)).start()
+
+        @pl.when(step == 0)
+        def _():
+            turn(other)
 
         @pl.when(step > 0)
         def _():
             awaited(3, step).wait_recv()
 
-        mirror[step] = mix(up_h, up_l, row_field[step], left)
+        mirror[step] = mix(upward, row_field[step], left)
         for d, peer in enumerate(row_peers):
             copy(2, step, mirror.at[step, block(peer)], mirror_in.at[step, d], (peer, c)).start()
         image = jnp.where(left, product(*diag_left, own), product(*diag_right, own))
@@ -248,8 +264,7 @@
     rows, cols = half * orb, n_row * orb
     hbm = pl.BlockSpec(memory_space=pl.ANY)
     f32, bf16, i32 = jnp.float32, jnp.bfloat16, jnp.int32
-    down = pltpu.VMEM((2, 2 * rows, cols), bf16)
-    upward = pltpu.VMEM((2, 2 * cols, rows), bf16)
+    tall, broad = up(rows, 128), up(cols, 128)
     return pl.pallas_call(
         functools.partial(kernel, n_row, n_col),
         out_shape=jax.ShapeDtypeStruct((2 * rows, width), f32),
@@ -263,8 +278,9 @@
             pltpu.VMEM((2, stored, orb, orb), f32),
             pltpu.VMEM((2, orb, orb), f32),
             pltpu.VMEM((2, stored // 2, orb, width), f32),
-            pltpu.VMEM((2, up(rows, 128), up(cols, 128)), f32),
-            down, down, upward, upward,
+            pltpu.VMEM((2, tall, broad), f32),
+            pltpu.VMEM((2 * rows, 4 * broad), bf16),
+            pltpu.VMEM((2 * cols, 4 * tall), bf16),
             pltpu.VMEM((DEGREE, cols, width), f32),
             pltpu.VMEM((DEGREE, rows, width), f32),
             pltpu.VMEM((2, rows, width), f32),

time: 45 us -> 44.9 us (level)
  no operation moved by 1% of the time
where the time goes in v4:
time: 44.9 us; the launch traced here: 44.7 us
  Pallas kernels  43.1 us (96%)
  local copies, waits for them, and re-layouts  1.64 us (4%)
    pallas_call x1, Pallas kernels, body(): pl.pallas_call(functools.partial(kernel, n_row, n_col), out_shape=jax.Sha...  43.1 us
    unnamed x1, local copies, waits for them, and re-layouts  1.64 us

profile of v4, /device:TPU:0, one launch (start us, length us, event | category | flops | bytes accessed | tf_op | source)
XLA Modules:
  0.0 44.7 jit_solution(9270718909765845158)
XLA Ops:
  0.0 43.1 %shard_map.46 = f32[448,128]{1,0:T(8,128)} custom-call(s32[2,10]{1,0:T(2,128)} %bitcast.5, f32[448,128]{1,0:T(8,128)} %vectors_hbm.1, f32[10,56,56]{2,1,0:T(8,128)} %bitcast.3, f32[56,56]{1,0:T(8,128)} %bitcast.4), custom_call_target="tpu_custom_call" | custom-call | flops 308281344 | bytes 229376 | tf_op jit(solution)/shard_map/pallas_call | solution.py:268
  43.1 1.6 %copy.6 = f32[448,128]{1,0:T(8,128)} copy(f32[448,128]{1,0:T(8,128)} %shard_map.46) | data formatting | bytes 458752

commit v5 on v4

--- a/solution.py
+++ b/solution.py
@@ -23,6 +23,15 @@
     right_high, right_low = halves(right)
     dot = functools.partial(jnp.dot, preferred_element_type=jnp.float32)
     return dot(left_high, right_high) + (dot(left_high, right_low) + dot(left_low, right_high))
+
+
+def flipped(index, mask, extent):
+    bit = 1
+    while bit < extent:
+        if mask // bit % 2 == 1:
+            index = index + bit * (1 - 2 * (index // bit % 2))
+        bit *= 2
+    return index
 
 
 def mix(panels, field, left):
@@ -53,8 +62,8 @@
     h, m = c // half, c % half
     other = 1 - h
     partner = other * half + m
-    row_peers = [lax.rem(r + d, n_row) for d in range(1, n_row)]
-    col_slots = [lax.rem(m + d, half) for d in range(1, half)]
+    row_peers = [flipped(r, d, n_row) for d in range(n_row - 1, 0, -1)]
+    col_slots = [flipped(m, d, half) for d in range(half - 1, 0, -1)]
     left = lax.broadcasted_iota(jnp.int32, (1, width), 1) < width // 2
 
     def block(index):
@@ -117,6 +126,8 @@
         else:
             pieces.append(jnp.zeros((orb, part), jnp.float32))
         packed[0, k] = jnp.concatenate(pieces, axis=1)
+    pl.semaphore_wait(barrier, n_row + half - 1)
+    copy(4, 0, packed.at[0], packed.at[1], (r, partner)).start()
     loads[0].wait()
     at_row = lax.broadcasted_iota(jnp.int32, (n_col, 128), 0)
     at_col = lax.broadcasted_iota(jnp.int32, (n_col, 128), 1)
@@ -134,10 +145,7 @@
     own = row_field[0, block(m), :]
     col_field[0, block(r), :] = own
 
-    pl.semaphore_wait(barrier, n_row + half - 1)
-
     copy(4, 1, slots.at[0], slots.at[1], (r, partner)).start()
-    copy(4, 0, packed.at[0], packed.at[1], (r, partner)).start()
     for peer in row_peers:
         copy(0, 0, row_field.at[0, block(m)], col_field.at[0, block(r)], (peer, c)).start()
 
@@ -293,7 +301,7 @@
             pltpu.SemaphoreType.DMA((5, 4)),
         ],
         compiler_params=pltpu.CompilerParams(
-            collective_id=0, has_side_effects=True, vmem_limit_bytes=56 * 1024 * 1024
+            collective_id=0, has_side_effects=True, vmem_limit_bytes=54912 * 1024
         ),
         cost_estimate=pl.CostEstimate(
             flops=16 * DEGREE * rows * cols * width, bytes_accessed=8 * rows * width, transcendentals=0

time: 44.9 us -> 46.1 us (1.027)
  Pallas kernels: 43.1 us -> 43.8 us
  local copies, waits for them, and re-layouts: 1.64 us -> 2.12 us
    pallas_call x1, Pallas kernels: 43.1 us -> 43.8 us  [body(): pl.pallas_call(functools.partial(kernel, n_row, n_col), out_shape=jax.Sha...]
    unnamed x1 -> x5, local copies, waits for them, and re-layouts: 1.64 us -> 2.12 us
where the time goes in v5:
time: 46.1 us; the launch traced here: 45.9 us
  Pallas kernels  43.8 us (95%)
  local copies, waits for them, and re-layouts  2.12 us (5%)
    pallas_call x1, Pallas kernels, body(): pl.pallas_call(functools.partial(kernel, n_row, n_col), out_shape=jax.Sha...  43.8 us
    unnamed x5, local copies, waits for them, and re-layouts  2.12 us

profile of v5, /device:TPU:0, one launch (start us, length us, event | category | flops | bytes accessed | tf_op | source)
XLA Modules:
  0.0 45.9 jit_solution(8966162313159674103)
XLA Ops:
  0.0 0.0 copy-start.1
  0.0 0.7 %copy-done.1 = s32[1,1,2,10]{3,2,1,0:T(2,128)S(1)} copy-done((s32[1,1,2,10]{3,2,1,0:T(2,128)S(1)}, s32[1,1,2,10]{3,2,1,0:T(2,128)}, u32[]{:S(2)}) %copy-start.1) | copy-done | bytes 104
  0.7 0.0 copy-start
  0.7 0.7 %copy-done = f32[1,56,56]{2,1,0:T(8,128)S(1)} copy-done((f32[1,56,56]{2,1,0:T(8,128)S(1)}, f32[1,56,56]{2,1,0:T(8,128)}, u32[]{:S(2)}) %copy-start) | copy-done | bytes 12568
  1.4 43.8 %shard_map.46 = f32[448,128]{1,0:T(8,128)S(1)} custom-call(s32[2,10]{1,0:T(2,128)S(1)} %bitcast.4, f32[448,128]{1,0:T(8,128)} %vectors_hbm.1, f32[10,56,56]{2,1,0:T(8,128)} %bitcast.5, f32[56,56]{1,0:T(8,128)S(1)} %bitcast.3), custom_call_target="tpu_custom_call" | custom-call | flops 308281344 | bytes 229376 | tf_op jit(solution)/shard_map/pallas_call | solution.py:276
  45.2 0.7 %copy.6 = f32[448,128]{1,0:T(8,128)} copy(f32[448,128]{1,0:T(8,128)S(1)} %shard_map.46) | data formatting | bytes 458752
Async XLA Ops:
  0.0 0.7 %copy-start.1 = (s32[1,1,2,10]{3,2,1,0:T(2,128)S(1)}, s32[1,1,2,10]{3,2,1,0:T(2,128)}, u32[]{:S(2)}) copy-start(s32[1,1,2,10]{3,2,1,0:T(2,128)} %param.6) | copy-start | bytes 244
  0.7 0.7 %copy-start = (f32[1,56,56]{2,1,0:T(8,128)S(1)}, f32[1,56,56]{2,1,0:T(8,128)}, u32[]{:S(2)}) copy-start(f32[1,56,56]{2,1,0:T(8,128)} %param.7) | copy-start | bytes 37636

commit v6 on v4

--- a/solution.py
+++ b/solution.py
@@ -117,6 +117,8 @@
         else:
             pieces.append(jnp.zeros((orb, part), jnp.float32))
         packed[0, k] = jnp.concatenate(pieces, axis=1)
+    pl.semaphore_wait(barrier, n_row + half - 1)
+    copy(4, 0, packed.at[0], packed.at[1], (r, partner)).start()
     loads[0].wait()
     at_row = lax.broadcasted_iota(jnp.int32, (n_col, 128), 0)
     at_col = lax.broadcasted_iota(jnp.int32, (n_col, 128), 1)
@@ -134,10 +136,7 @@
     own = row_field[0, block(m), :]
     col_field[0, block(r), :] = own
 
-    pl.semaphore_wait(barrier, n_row + half - 1)
-
     copy(4, 1, slots.at[0], slots.at[1], (r, partner)).start()
-    copy(4, 0, packed.at[0], packed.at[1], (r, partner)).start()
     for peer in row_peers:
         copy(0, 0, row_field.at[0, block(m)], col_field.at[0, block(r)], (peer, c)).start()
 

time: 44.9 us -> 45.4 us (1.011)
  Pallas kernels: 43.1 us -> 43.6 us
    pallas_call x1, Pallas kernels: 43.1 us -> 43.6 us  [body(): pl.pallas_call(functools.partial(kernel, n_row, n_col), out_shape=jax.Sha...]
where the time goes in v6:
time: 45.4 us; the launch traced here: 45.3 us
  Pallas kernels  43.6 us (96%)
  local copies, waits for them, and re-layouts  1.64 us (4%)
    pallas_call x1, Pallas kernels, body(): pl.pallas_call(functools.partial(kernel, n_row, n_col), out_shape=jax.Sha...  43.6 us
    unnamed x1, local copies, waits for them, and re-layouts  1.64 us

profile of v6, /device:TPU:0, one launch (start us, length us, event | category | flops | bytes accessed | tf_op | source)
XLA Modules:
  0.0 45.3 jit_solution(5055470947584104490)
XLA Ops:
  0.0 43.6 %shard_map.46 = f32[448,128]{1,0:T(8,128)} custom-call(s32[2,10]{1,0:T(2,128)} %bitcast.5, f32[448,128]{1,0:T(8,128)} %vectors_hbm.1, f32[10,56,56]{2,1,0:T(8,128)} %bitcast.3, f32[56,56]{1,0:T(8,128)} %bitcast.4), custom_call_target="tpu_custom_call" | custom-call | flops 308281344 | bytes 229376 | tf_op jit(solution)/shard_map/pallas_call | solution.py:267
  43.6 1.6 %copy.6 = f32[448,128]{1,0:T(8,128)} copy(f32[448,128]{1,0:T(8,128)} %shard_map.46) | data formatting | bytes 458752

commit v7 on v3

--- a/solution.py
+++ b/solution.py
@@ -69,7 +69,8 @@
         pl.semaphore_signal(barrier, inc=1, device_id=(peer, c), device_id_type=MESH)
     for slot in col_slots:
         pl.semaphore_signal(barrier, inc=1, device_id=(r, h * half + slot), device_id_type=MESH)
-    pl.semaphore_signal(barrier, inc=1, device_id=(r, partner), device_id_type=MESH)
+    for slot in [m] + col_slots:
+        pl.semaphore_signal(barrier, inc=1, device_id=(r, other * half + slot), device_id_type=MESH)
 
     def copy(kind, step, source, target, device):
         return pltpu.make_async_remote_copy(
@@ -87,13 +88,11 @@
             return mirror_in.at[step]
         if kind == 3:
             return row_field.at[step, pl.ds(0, rows - orb)]
-        if step == 3:
-            return final.at[0, pl.ds(0, rows - orb)]
         if step == 0:
             return packed.at[1]
         if step == 1:
             return slots.at[1]
-        return final.at[0, pl.ds(0, orb)]
+        return final.at[0]
 
     def awaited(kind, step):
         region = region_of(kind, step)
@@ -129,7 +128,7 @@
     own = row_field[0, block(m), :]
     col_field[0, block(r), :] = own
 
-    pl.semaphore_wait(barrier, n_row + half - 1)
+    pl.semaphore_wait(barrier, n_row + n_col - 2)
 
     copy(4, 1, slots.at[0], slots.at[1], (r, partner)).start()
     copy(4, 0, packed.at[0], packed.at[1], (r, partner)).start()
@@ -218,21 +217,19 @@
         return own, following
 
     _, own = lax.fori_loop(0, DEGREE, one_step, (jnp.zeros_like(own), own))
-    final[h, block(m), :] = own
-    mine, theirs = final.at[h, block(m)], final.at[other, block(m)]
-    copy(4, 2, mine, mine, (r, partner)).start()
+    final[h, block(m), :] = 0.5 * own
+    mine = final.at[h, block(m)]
+    for slot in [m] + col_slots:
+        copy(4, 2, mine, mine, (r, other * half + slot)).start()
     for slot in col_slots:
         copy(3, 0, mine, mine, (r, h * half + slot)).start()
+    awaited(3, 0).wait_recv()
     awaited(4, 2).wait_recv()
-    for slot in col_slots:
-        copy(4, 3, theirs, theirs, (r, h * half + slot)).start()
-    awaited(3, 0).wait_recv()
-    awaited(4, 3).wait_recv()
     low, high = final[0], final[1]
     out_ref[pl.ds(0, rows), :] = jnp.where(left, low, pltpu.roll(high, width // 2, 1))
     out_ref[pl.ds(rows, rows), :] = jnp.where(left, pltpu.roll(low, width // 2, 1), high)
     for kind in range(5):
-        for step in range(4 if kind == 4 else DEGREE):
+        for step in range(DEGREE):
             awaited(kind, step).wait_send()
 
 
@@ -250,7 +247,7 @@
     f32, bf16, i32 = jnp.float32, jnp.bfloat16, jnp.int32
     down = pltpu.VMEM((2, 2 * rows, cols), bf16)
     upward = pltpu.VMEM((2, 2 * cols, rows), bf16)
-    return pl.pallas_call(
+    halved = pl.pallas_call(
         functools.partial(kernel, n_row, n_col),
         out_shape=jax.ShapeDtypeStruct((2 * rows, width), f32),
         in_specs=[hbm, hbm, hbm, hbm],
@@ -283,6 +280,7 @@
             flops=16 * DEGREE * rows * cols * width, bytes_accessed=8 * rows * width, transcendentals=0
         ),
     )(tile_pos[0, 0], vectors, tile_data, diag_blocks[0])
+    return 2.0 * halved
 
 
 def solution(mesh):

time: 45 us -> 45.9 us (1.020)
  other arithmetic: 0 us -> 1.64 us
  local copies, waits for them, and re-layouts: 1.64 us -> 0 us
  Pallas kernels: 43.2 us -> 44.1 us
    mul x0 -> x1, other arithmetic: none -> 1.64 us  [body(): return 2.0 * halved]
    unnamed x1 -> x0, local copies, waits for them, and re-layouts: 1.64 us -> none
    pallas_call x1, Pallas kernels: 43.2 us -> 44.1 us  [body(): pl.pallas_call(functools.partial(kernel, n_row, n_col), out_shape=jax.Sha...]
where the time goes in v7:
time: 45.9 us; the launch traced here: 45.8 us
  Pallas kernels  44.1 us (96%)
  other arithmetic  1.64 us (4%)
    pallas_call x1, Pallas kernels, body(): pl.pallas_call(functools.partial(kernel, n_row, n_col), out_shape=jax.Sha...  44.1 us
    mul x1, other arithmetic, body(): return 2.0 * halved  1.64 us

profile of v7, /device:TPU:0, one launch (start us, length us, event | category | flops | bytes accessed | tf_op | source)
XLA Modules:
  0.0 45.8 jit_solution(7310831331027887158)
XLA Ops:
  0.0 44.1 %shard_map.46 = f32[448,128]{1,0:T(8,128)} custom-call(s32[2,10]{1,0:T(2,128)} %bitcast.5, f32[448,128]{1,0:T(8,128)} %vectors_hbm.1, f32[10,56,56]{2,1,0:T(8,128)} %bitcast.3, f32[56,56]{1,0:T(8,128)} %bitcast.4), custom_call_target="tpu_custom_call" | custom-call | flops 308281344 | bytes 229376 | tf_op jit(solution)/shard_map/pallas_call | solution.py:250
  44.1 1.6 %broadcast_multiply_fusion = f32[448,128]{1,0:T(8,128)} fusion(f32[448,128]{1,0:T(8,128)} %shard_map.46), kind=kLoop, calls=%fused_computation | loop fusion | flops 57344 | bytes 458752 | tf_op jit(solution)/shard_map/mul | solution.py:283

commit v8 on v4

--- a/solution.py
+++ b/solution.py
@@ -26,13 +26,18 @@
 
 
 def mix(panels, field, left):
-    far = pltpu.roll(field, field.shape[1] // 2, 1)
+    count, width = field.shape
     depth = panels.shape[1] // 4
-    empty = jnp.zeros((depth - field.shape[0], field.shape[1]), jnp.float32)
-    pieces = [field, far] if depth == field.shape[0] else [field, empty, far, empty]
-    high, low = halves(jnp.concatenate(pieces, axis=0))
-    dot = functools.partial(jnp.dot, preferred_element_type=jnp.float32)
-    both = dot(panels[...], jnp.concatenate([high, high], axis=0)) + dot(panels[:, pl.ds(0, 2 * depth)], low)
+    turn = functools.partial(pltpu.roll, shift=width // 2, axis=1)
+    high = field.astype(jnp.bfloat16).astype(jnp.float32)
+    low = field - high
+    pieces = [jnp.where(left, high, turn(low)), jnp.where(left, turn(high), low)]
+    if depth > count:
+        empty = jnp.zeros((depth - count, width), jnp.float32)
+        pieces = [pieces[0], empty, pieces[1], empty]
+    right = jnp.concatenate(pieces, axis=0).astype(jnp.bfloat16)
+    both = jnp.dot(panels[...], jnp.concatenate([right, right], axis=0), preferred_element_type=jnp.float32)
+    both = both + turn(both)
     count = both.shape[0] // 2
     return jnp.where(left, both[:count], both[count:])
 
@@ -156,18 +161,18 @@
                 return carry
 
             lax.fori_loop(0, half, one, 0)
-            put(down, place if a == 0 else 1 - place, pl.ds(a * rows, rows), dense[a, pl.ds(0, rows), :])
-
-    def put(panels, turned, there, panel):
+            put(down, place, pl.ds(a * rows, rows), dense[a, pl.ds(0, rows), :])
+
+    def put(panels, part, there, panel):
         depth = panel.shape[1]
         high, low = halves(panel)
-        panels[there, pl.ds(pl.multiple_of(turned * depth, 128), depth)] = high
-        panels[there, pl.ds(pl.multiple_of((turned + 2) * depth, 128), depth)] = low
+        panels[there, pl.ds(pl.multiple_of(part * depth, 128), depth)] = high
+        panels[there, pl.ds(pl.multiple_of((part + 2) * depth, 128), depth)] = low
 
     def turn(place):
         there = pl.ds(pl.multiple_of(place * cols, 16), cols)
         for a in range(2):
-            put(upward, place if a == 0 else 1 - place, there, dense[a].T[:cols])
+            put(upward, a, there, dense[a].T[:cols])
 
     fill(0, h)
     turn(h)

time: 44.9 us -> 44.4 us (0.989)
  Pallas kernels: 43.1 us -> 42.6 us
    pallas_call x1, Pallas kernels: 43.1 us -> 42.6 us  [body(): pl.pallas_call(functools.partial(kernel, n_row, n_col), out_shape=jax.Sha...]
where the time goes in v8:
time: 44.4 us; the launch traced here: 44.3 us
  Pallas kernels  42.6 us (96%)
  local copies, waits for them, and re-layouts  1.64 us (4%)
    pallas_call x1, Pallas kernels, body(): pl.pallas_call(functools.partial(kernel, n_row, n_col), out_shape=jax.Sha...  42.6 us
    unnamed x1, local copies, waits for them, and re-layouts  1.64 us

profile of v8, /device:TPU:0, one launch (start us, length us, event | category | flops | bytes accessed | tf_op | source)
XLA Modules:
  0.0 44.3 jit_solution(6692063829158230965)
XLA Ops:
  0.0 42.6 %shard_map.46 = f32[448,128]{1,0:T(8,128)} custom-call(s32[2,10]{1,0:T(2,128)} %bitcast.5, f32[448,128]{1,0:T(8,128)} %vectors_hbm.1, f32[10,56,56]{2,1,0:T(8,128)} %bitcast.3, f32[56,56]{1,0:T(8,128)} %bitcast.4), custom_call_target="tpu_custom_call" | custom-call | flops 308281344 | bytes 229376 | tf_op jit(solution)/shard_map/pallas_call | solution.py:273
  42.6 1.6 %copy.6 = f32[448,128]{1,0:T(8,128)} copy(f32[448,128]{1,0:T(8,128)} %shard_map.46) | data formatting | bytes 458752

commit v9 on v8

--- a/solution.py
+++ b/solution.py
@@ -88,6 +88,9 @@
             device_id=device, device_id_type=MESH,
         )
 
+    cut = orb // 16 * 8
+    shares = ((0, cut), (cut, orb - cut))
+
     def region_of(kind, step):
         if kind == 0:
             return col_field.at[step, pl.ds(0, cols - orb)]
@@ -97,13 +100,12 @@
             return mirror_in.at[step]
         if kind == 3:
             return row_field.at[step, pl.ds(0, rows - orb)]
-        if step == 3:
-            return final.at[0, pl.ds(0, rows - orb)]
         if step == 0:
             return packed.at[1]
         if step == 1:
             return slots.at[1]
-        return final.at[0, pl.ds(0, orb)]
+        size = shares[step // 2 - 1][1]
+        return final.at[0, pl.ds(0, size * (half - 1 if step % 2 == 1 else 1))]
 
     def awaited(kind, step):
         region = region_of(kind, step)
@@ -240,20 +242,25 @@
 
     _, own = lax.fori_loop(0, DEGREE, one_step, (jnp.zeros_like(own), own))
     final[h, block(m), :] = own
-    mine, theirs = final.at[h, block(m)], final.at[other, block(m)]
-    copy(4, 2, mine, mine, (r, partner)).start()
+    mine = final.at[h, block(m)]
+    for kind, (start, size) in zip((2, 4), shares):
+        piece = final.at[h, pl.ds(pl.multiple_of(m * orb + start, 8), size)]
+        copy(4, kind, piece, piece, (r, partner)).start()
     for slot in col_slots:
         copy(3, 0, mine, mine, (r, h * half + slot)).start()
-    awaited(4, 2).wait_recv()
-    for slot in col_slots:
-        copy(4, 3, theirs, theirs, (r, h * half + slot)).start()
+    for kind, (start, size) in zip((2, 4), shares):
+        piece = final.at[other, pl.ds(pl.multiple_of(m * orb + start, 8), size)]
+        awaited(4, kind).wait_recv()
+        for slot in col_slots:
+            copy(4, kind + 1, piece, piece, (r, h * half + slot)).start()
     awaited(3, 0).wait_recv()
     awaited(4, 3).wait_recv()
+    awaited(4, 5).wait_recv()
     low, high = final[0], final[1]
     out_ref[pl.ds(0, rows), :] = jnp.where(left, low, pltpu.roll(high, width // 2, 1))
     out_ref[pl.ds(rows, rows), :] = jnp.where(left, pltpu.roll(low, width // 2, 1), high)
     for kind in range(5):
-        for step in range(4 if kind == 4 else DEGREE):
+        for step in range(6 if kind == 4 else DEGREE):
             awaited(kind, step).wait_send()
 
 
@@ -294,8 +301,8 @@
             pltpu.VMEM((DEGREE, half - 1, orb, width), f32),
             pltpu.VMEM((DEGREE, n_row - 1, orb, width), f32),
             pltpu.SemaphoreType.DMA((6,)),
-            pltpu.SemaphoreType.DMA((5, 4)),
-            pltpu.SemaphoreType.DMA((5, 4)),
+            pltpu.SemaphoreType.DMA((5, 6)),
+            pltpu.SemaphoreType.DMA((5, 6)),
         ],
         compiler_params=pltpu.CompilerParams(
             collective_id=0, has_side_effects=True, vmem_limit_bytes=56 * 1024 * 1024

time: 44.4 us -> 44.5 us (level)
  no operation moved by 1% of the time
where the time goes in v9:
time: 44.5 us; the launch traced here: 44.3 us
  Pallas kernels  42.7 us (96%)
  local copies, waits for them, and re-layouts  1.64 us (4%)
    pallas_call x1, Pallas kernels, body(): pl.pallas_call(functools.partial(kernel, n_row, n_col), out_shape=jax.Sha...  42.7 us
    unnamed x1, local copies, waits for them, and re-layouts  1.64 us

profile of v9, /device:TPU:0, one launch (start us, length us, event | category | flops | bytes accessed | tf_op | source)
XLA Modules:
  0.0 44.3 jit_solution(8500927076641057510)
XLA Ops:
  0.0 42.7 %shard_map.46 = f32[448,128]{1,0:T(8,128)} custom-call(s32[2,10]{1,0:T(2,128)} %bitcast.5, f32[448,128]{1,0:T(8,128)} %vectors_hbm.1, f32[10,56,56]{2,1,0:T(8,128)} %bitcast.3, f32[56,56]{1,0:T(8,128)} %bitcast.4), custom_call_target="tpu_custom_call" | custom-call | flops 308281344 | bytes 229376 | tf_op jit(solution)/shard_map/pallas_call | solution.py:280
  42.7 1.6 %copy.6 = f32[448,128]{1,0:T(8,128)} copy(f32[448,128]{1,0:T(8,128)} %shard_map.46) | data formatting | bytes 458752

commit v10 on v9

--- a/solution.py
+++ b/solution.py
@@ -233,10 +233,11 @@
             row_field[step + 1, block(m), :] = following
             col_field[step + 1, block(r), :] = following
             mine = row_field.at[step + 1, block(m)]
-            for peer in row_peers:
-                copy(0, step + 1, mine, col_field.at[step + 1, block(r)], (peer, c)).start()
-            for slot in col_slots:
-                copy(3, step + 1, mine, mine, (r, h * half + slot)).start()
+            for d in range(max(len(row_peers), len(col_slots))):
+                if d < len(row_peers):
+                    copy(0, step + 1, mine, col_field.at[step + 1, block(r)], (row_peers[d], c)).start()
+                if d < len(col_slots):
+                    copy(3, step + 1, mine, mine, (r, h * half + col_slots[d])).start()
 
         return own, following
 

time: 44.5 us -> 44.5 us (level)
  no operation moved by 1% of the time
where the time goes in v10:
time: 44.5 us; the launch traced here: 44.3 us
  Pallas kernels  42.6 us (96%)
  local copies, waits for them, and re-layouts  1.64 us (4%)
    pallas_call x1, Pallas kernels, body(): pl.pallas_call(functools.partial(kernel, n_row, n_col), out_shape=jax.Sha...  42.6 us
    unnamed x1, local copies, waits for them, and re-layouts  1.64 us

profile of v10, /device:TPU:0, one launch (start us, length us, event | category | flops | bytes accessed | tf_op | source)
XLA Modules:
  0.0 44.3 jit_solution(1215385098855065906)
XLA Ops:
  0.0 42.6 %shard_map.46 = f32[448,128]{1,0:T(8,128)} custom-call(s32[2,10]{1,0:T(2,128)} %bitcast.5, f32[448,128]{1,0:T(8,128)} %vectors_hbm.1, f32[10,56,56]{2,1,0:T(8,128)} %bitcast.3, f32[56,56]{1,0:T(8,128)} %bitcast.4), custom_call_target="tpu_custom_call" | custom-call | flops 308281344 | bytes 229376 | tf_op jit(solution)/shard_map/pallas_call | solution.py:281
  42.7 1.6 %copy.6 = f32[448,128]{1,0:T(8,128)} copy(f32[448,128]{1,0:T(8,128)} %shard_map.46) | data formatting | bytes 458752
